TPU v7x, 32 devices: a whole 2x2x4 slice. The times are simulated.
32 devices in a mesh: sweep: 4 (over y, x), azim: 8 (over z, core).
Axes of the slice: x: 2, y: 2, z: 4, core: 2. Of those that a mesh axis runs over, the one named last changes fastest.
Arguments:
- latents: bfloat16 [8, 8, 256, 512], P('sweep', None, 'azim'), may hold values from -6 to 6
- cotangent: bfloat16 [8, 8, 256, 512], P('sweep', None, 'azim'), may hold values from -6 to 6
- conv_kernel: float32 [9, 512], replicated, may hold values from -2 to 2
- conv_bias: float32 [512], replicated, may hold values from -3 to 3
- norm_gain: float32 [512], replicated, may hold values from 0.25 to 1.75
- w_query: bfloat16 [512, 256], replicated, may hold values from -2 to 2
- w_key: bfloat16 [512, 256], replicated, may hold values from -2 to 2
- w_value: bfloat16 [512, 256], replicated, may hold values from -0.25 to 0.25
- w_output: bfloat16 [512, 256], replicated, may hold values from -0.375 to 0.375
Outputs:
- grad_latents: float32 [8, 8, 256, 512], P('sweep', None, 'azim')
- grad_kernel: float32 [9, 512], replicated
- grad_bias: float32 [512], replicated
- grad_gain: float32 [512], replicated
- grad_query: float32 [512, 256], P('azim')
- grad_key: float32 [512, 256], P('azim')
- grad_value: float32 [512, 256], P('azim')
- grad_output: float32 [512, 256], P('azim')
All inputs are finite; a program needn't handle non-finite values.
Results may differ from a plain program's by a relative error of at most 0.01.
The roundings to bfloat16 on the way count: a program that leaves them out, or rounds other values in their place, can miss the bound.
Values may be sent and summed in bfloat16 or wider, within the bound.
A program may use at most 64 MiB of HBM per device.

v0:
```python
import math

import jax
import jax.numpy as jnp
from jax import lax
from jax.sharding import PartitionSpec as P

DH = 64


EPS = 1e-06


def extended(value, sides, width):
    for axis, dim in sides:
        size, length = (lax.axis_size(axis), value.shape[dim])
        up = [(i, (i + 1) % size) for i in range(size)]
        down = [(j, i) for i, j in up]
        last = lax.slice_in_dim(value, length - width, length, axis=dim)
        leading = lax.slice_in_dim(value, 0, width, axis=dim)
        before = lax.ppermute(last, axis, up)
        after = lax.ppermute(leading, axis, down)
        value = jnp.concatenate([before, value, after], axis=dim)
    return value


def silu_slope(value):
    sigmoid_val = jax.nn.sigmoid(value)
    return sigmoid_val * (1.0 + value * (1.0 - sigmoid_val))


def outer_sum(left, right):
    return lax.dot_general(
        left, right, (((0,), (0,)), ((), ())), preferred_element_type=jnp.float32
    )


def attend(y_block, cot_block, w_query, w_key, w_value, w_output, norm_gain):
    sweeps, pixels, channels = y_block.shape
    heads = w_query.shape[1] // DH
    scale = 1.0 / math.sqrt(DH)
    y_float = y_block.astype(jnp.float32)
    root = jnp.sqrt(jnp.mean(y_float * y_float, axis=-1, keepdims=True) + EPS)
    inverse = 1.0 / root
    normed = (y_float * inverse * norm_gain).astype(jnp.bfloat16)
    rows = normed.reshape(sweeps * pixels, channels)
    query = jnp.dot(rows, w_query, preferred_element_type=jnp.float32).astype(jnp.bfloat16)
    key = jnp.dot(rows, w_key, preferred_element_type=jnp.float32).astype(jnp.bfloat16)
    value = jnp.dot(rows, w_value, preferred_element_type=jnp.float32).astype(jnp.bfloat16)
    query4 = query.reshape(sweeps, pixels, heads, DH)
    key4 = key.reshape(sweeps, pixels, heads, DH)
    value4 = value.reshape(sweeps, pixels, heads, DH)
    scores = jnp.einsum("tphd,uphd->phtu", query4, key4, preferred_element_type=jnp.float32) * scale
    row_max = jnp.max(scores, axis=-1, keepdims=True)
    expon = jnp.exp(scores - row_max)
    probs = expon / jnp.sum(expon, axis=-1, keepdims=True)
    probs_low = probs.astype(jnp.bfloat16)
    attended = jnp.einsum(
        "phtu,uphd->tphd", probs_low, value4, preferred_element_type=jnp.float32
    ).astype(jnp.bfloat16)
    attended_rows = attended.reshape(sweeps * pixels, heads * DH)
    cot_rows = cot_block.reshape(sweeps * pixels, channels)
    grad_output = outer_sum(cot_rows, attended_rows)
    grad_attended = jnp.dot(cot_rows, w_output, preferred_element_type=jnp.float32).astype(
        jnp.bfloat16
    )
    grad_att4 = grad_attended.reshape(sweeps, pixels, heads, DH)
    grad_probs = jnp.einsum(
        "tphd,uphd->phtu", grad_att4, value4, preferred_element_type=jnp.float32
    )
    grad_scores = (
        probs * (grad_probs - jnp.sum(probs * grad_probs, axis=-1, keepdims=True)) * scale
    ).astype(jnp.bfloat16)
    grad_v = jnp.einsum(
        "phtu,tphd->uphd", probs_low, grad_att4, preferred_element_type=jnp.float32
    ).astype(jnp.bfloat16)
    grad_q = jnp.einsum(
        "phtu,uphd->tphd", grad_scores, key4, preferred_element_type=jnp.float32
    ).astype(jnp.bfloat16)
    grad_k = jnp.einsum(
        "phtu,tphd->uphd", grad_scores, query4, preferred_element_type=jnp.float32
    ).astype(jnp.bfloat16)
    grad_q = grad_q.reshape(sweeps * pixels, heads * DH)
    grad_k = grad_k.reshape(sweeps * pixels, heads * DH)
    grad_v = grad_v.reshape(sweeps * pixels, heads * DH)
    grad_query = outer_sum(rows, grad_q)
    grad_key = outer_sum(rows, grad_k)
    grad_value = outer_sum(rows, grad_v)
    stacked_grads = jnp.concatenate([grad_q, grad_k, grad_v], axis=-1)
    stacked_weights = jnp.concatenate([w_query, w_key, w_value], axis=-1)
    grad_normed = lax.dot_general(
        stacked_grads, stacked_weights, (((1,), (1,)), ((), ())), preferred_element_type=jnp.float32
    )
    grad_normed = grad_normed.reshape(sweeps, pixels, channels)
    grad_gain = jnp.sum(grad_normed * y_float * inverse, axis=(0, 1))
    gained = grad_normed * norm_gain
    grad_attn = (
        inverse
        * (
            gained
            - y_float * jnp.mean(gained * y_float, axis=-1, keepdims=True) * inverse * inverse
        )
    ).astype(jnp.bfloat16)
    return (grad_attn, grad_query, grad_key, grad_value, grad_output, grad_gain)


def on_device(
    latents, cotangent, conv_kernel, conv_bias, norm_gain, w_query, w_key, w_value, w_output
):
    sweep_local, height, azim_local, channels = latents.shape
    groups = lax.axis_size("sweep")
    strips = lax.axis_size("azim")
    pixels_each = height * azim_local // groups
    framed = extended(latents, (("azim", 2),), 1)
    activation = jnp.pad(jax.nn.silu(framed.astype(jnp.float32)), ((0, 0), (1, 1), (0, 0), (0, 0)))
    conv_sum = jnp.zeros(latents.shape, jnp.float32)
    for row_tap in range(3):
        for col_tap in range(3):
            conv_sum = (
                conv_sum
                + conv_kernel[3 * row_tap + col_tap]
                * activation[:, row_tap : row_tap + height, col_tap : col_tap + azim_local]
            )
    y_local = (latents.astype(jnp.float32) + conv_sum + conv_bias).astype(jnp.bfloat16)
    y_split = y_local.reshape(sweep_local, groups, pixels_each, channels)
    cot_split = cotangent.reshape(sweep_local, groups, pixels_each, channels)
    y_pix, cot_pix = (
        lax.all_to_all(y_split, "sweep", split_axis=1, concat_axis=0, tiled=True),
        lax.all_to_all(cot_split, "sweep", split_axis=1, concat_axis=0, tiled=True),
    )
    total_sweeps = sweep_local * groups
    y_pix = y_pix.reshape(total_sweeps, pixels_each, channels)
    cot_pix = cot_pix.reshape(total_sweeps, pixels_each, channels)
    grad_attn, grad_query, grad_key, grad_value, grad_output, grad_gain = attend(
        y_pix, cot_pix, w_query, w_key, w_value, w_output, norm_gain
    )
    returned = lax.all_to_all(
        grad_attn.reshape(total_sweeps, 1, pixels_each, channels),
        "sweep",
        split_axis=0,
        concat_axis=1,
        tiled=True,
    )
    returned = returned.reshape(sweep_local, height, azim_local, channels)
    grad_y = cotangent.astype(jnp.float32) + returned.astype(jnp.float32)
    framed_grad = extended(grad_y, (("azim", 2),), 1)
    framed_grad = jnp.pad(framed_grad, ((0, 0), (1, 1), (0, 0), (0, 0)))
    grad_act = jnp.zeros(grad_y.shape, jnp.float32)
    taps = []
    for row_tap in range(3):
        for col_tap in range(3):
            weight = conv_kernel[3 * row_tap + col_tap]
            grad_act = (
                grad_act
                + weight
                * framed_grad[
                    :, 2 - row_tap : 2 - row_tap + height, 2 - col_tap : 2 - col_tap + azim_local
                ]
            )
            taps.append(
                jnp.sum(
                    grad_y
                    * activation[:, row_tap : row_tap + height, col_tap : col_tap + azim_local],
                    axis=(0, 1, 2),
                )
            )
    latent_float = latents.astype(jnp.float32)
    grad_latents = grad_y + grad_act * silu_slope(latent_float)
    predivide = 1.0 / math.sqrt(total_sweeps * height * azim_local * strips)
    tap_terms = jnp.stack(taps) * predivide
    bias_terms = jnp.sum(grad_y, axis=(0, 1, 2)) * predivide
    gain_terms = grad_gain * predivide
    query_terms = grad_query * predivide
    key_terms = grad_key * predivide
    value_terms = grad_value * predivide
    output_terms = grad_output * predivide
    summed = lax.psum((query_terms, key_terms, value_terms, output_terms), ("sweep", "azim"))
    rows_each = channels // strips
    start = lax.axis_index("azim") * rows_each
    shares = tuple((lax.dynamic_slice_in_dim(whole, start, rows_each, 0) for whole in summed))
    grad_kernel, grad_bias, gain_total = lax.psum(
        (tap_terms, bias_terms, gain_terms), ("sweep", "azim")
    )
    return (
        grad_latents,
        grad_kernel,
        grad_bias,
        gain_total,
        shares[0],
        shares[1],
        shares[2],
        shares[3],
    )


def solution(mesh):
    in_specs = (
        P("sweep", None, "azim", None),
        P("sweep", None, "azim", None),
        P(),
        P(),
        P(),
        P(),
        P(),
        P(),
        P(),
    )
    out_specs = (
        P("sweep", None, "azim", None),
        P(),
        P(),
        P(),
        P("azim", None),
        P("azim", None),
        P("azim", None),
        P("azim", None),
    )
    return jax.shard_map(
        on_device, mesh=mesh, in_specs=in_specs, out_specs=out_specs, check_vma=False
    )
```

profile of v0, /device:TPU:0, one launch (start us, length us, event | category | flops | bytes accessed | tf_op | source)
XLA Modules:
  0.0 242.3 jit_solution(2077280573348472586)
XLA Ops:
  7.2 1.1 fusion.91
  8.8 4.1 %collective-permute-start.1 = (bf16[2,8,1,512]{3,2,1,0:T(2,128)(2,1)S(1)}, bf16[2,8,1,512]{3,2,1,0:T(2,128)(2,1)S(1)}, u32[]{:S(2)}, u32[]{:S(2)}) collective-permute-start(bf16[2,8,1,512]{3,2,1,0:T(2,128)(2,1)S(1)} %get-tuple-element.63), channel_id=1, source_target_pairs={{1,0},{2,1},{3,2},{4,3},{5,4},{6,5},{7,6},{0,7},{9,8},{10,9},{11,1... | collective-permute-start | bytes 49160 | tf_op jit(solution)/shard_map/ppermute | solution.py:22
  12.9 1.9 copy.68
  14.8 4.3 %all-to-all-start.1 = ((bf16[2,4,64,512]{3,2,0,1:T(8,128)(2,1)}), bf16[2,4,64,512]{3,2,0,1:T(8,128)(2,1)S(1)}, u32[]{:S(2)}, u32[]{:S(2)}) async-start(bf16[2,4,64,512]{3,2,0,1:T(8,128)(2,1)} %copy.68), calls=%async_computation.1 | async-start | bytes 1048576 | tf_op jit(solution)/shard_map/all_to_all | solution.py:129
  19.6 0.9 fusion.18
  20.5 0.8 copy.65
  21.3 4.3 %all-to-all-done.1 = bf16[2,4,64,512]{3,2,0,1:T(8,128)(2,1)S(1)} async-done(((bf16[2,4,64,512]{3,2,0,1:T(8,128)(2,1)}), bf16[2,4,64,512]{3,2,0,1:T(8,128)(2,1)S(1)}, u32[]{:S(2)}, u32[]{:S(2)}) %all-to-all-start.1) | async-done | bytes 524320 | tf_op jit(solution)/shard_map/all_to_all | solution.py:129
  25.6 3.5 %all-to-all-start = ((bf16[2,4,64,512]{3,2,0,1:T(8,128)(2,1)}), bf16[2,4,64,512]{3,2,0,1:T(8,128)(2,1)S(1)}, u32[]{:S(2)}, u32[]{:S(2)}) async-start(bf16[2,4,64,512]{3,2,0,1:T(8,128)(2,1)} %copy.65), calls=%async_computation | async-start | bytes 1048576 | tf_op jit(solution)/shard_map/all_to_all | solution.py:128
  29.4 1.0 reshape.203
  30.5 5.2 %all-to-all-done = bf16[2,4,64,512]{3,2,0,1:T(8,128)(2,1)S(1)} async-done(((bf16[2,4,64,512]{3,2,0,1:T(8,128)(2,1)}), bf16[2,4,64,512]{3,2,0,1:T(8,128)(2,1)S(1)}, u32[]{:S(2)}, u32[]{:S(2)}) %all-to-all-start) | async-done | bytes 524320 | tf_op jit(solution)/shard_map/all_to_all | solution.py:128
  36.2 1.2 convolution_convert_fusion.7
  37.4 1.0 reshape.200
  38.4 1.2 convolution_convert_fusion.6
  39.7 1.1 reshape.201
  40.8 1.2 convolution_convert_fusion.4
  42.0 1.1 reshape.204
  43.1 3.4 %fusion.93 = (f32[64,4,8]{2,1,0:T(4,128)S(1)}, f32[64,4,8,8]{2,3,1,0:T(8,128)}) fusion(bf16[8,64,4,64]{3,2,1,0:T(4,128)(2,1)} %reshape.200, bf16[8,64,4,64]{3,2,1,0:T(4,128)(2,1)} %reshape.201), kind=kOutput, calls=%fused_computation.145 | convolution fusion | flops 2146311 | bytes 598016 | tf_op jit(solution)/shard_map/sub | solution.py:55
  46.5 2.9 %fusion.67 = f32[64,4,8,8]{2,3,1,0:T(8,128)} fusion(bf16[8,64,4,64]{3,2,1,0:T(4,128)(2,1)} %reshape.204, bf16[8,64,4,64]{3,2,1,0:T(4,128)(2,1)S(1)} %copy-done.5), kind=kOutput, calls=%fused_computation.118 | convolution fusion | flops 2097152 | bytes 589824 | tf_op jit(solution)/shard_map/tphd,uphd->phtu/dot_general | solution.py:68
  49.3 1.4 fusion.15
  50.7 4.0 %fusion.12 = bf16[8,64,4,64]{3,0,2,1:T(8,128)(2,1)} fusion(f32[64,4,8,8]{2,3,1,0:T(8,128)} %fusion.67, bf16[8,64,4,64]{3,2,1,0:T(4,128)(2,1)} %reshape.200, f32[64,4,8,8]{2,3,1,0:T(8,128)} %get-tuple-element.74, f32[64,4,8]{2,1,0:T(4,128)S(1)} %get-tuple-element.73), kind=kOutput, calls=%fused_computation.32 | convolution fusion | flops 2344967 | bytes 663552 | tf_op jit(solution)/shard_map/phtu,uphd->tphd/dot_general | solution.py:77
  54.7 4.0 %fusion.13 = bf16[8,64,4,64]{3,0,2,1:T(8,128)(2,1)} fusion(f32[64,4,8,8]{2,3,1,0:T(8,128)} %fusion.67, bf16[8,64,4,64]{3,2,1,0:T(4,128)(2,1)} %reshape.201, f32[64,4,8,8]{2,3,1,0:T(8,128)} %get-tuple-element.74, f32[64,4,8]{2,1,0:T(4,128)S(1)} %get-tuple-element.73), kind=kOutput, calls=%fused_computation.33 | convolution fusion | flops 2344967 | bytes 663552 | tf_op jit(solution)/shard_map/phtu,tphd->uphd/dot_general | solution.py:80
  58.6 2.6 %fusion.14 = bf16[8,64,4,64]{3,0,2,1:T(8,128)(2,1)} fusion(bf16[8,64,4,64]{3,2,1,0:T(4,128)(2,1)S(1)} %copy-done.5, f32[64,4,8,8]{2,3,1,0:T(8,128)} %get-tuple-element.74, f32[64,4,8]{2,1,0:T(4,128)S(1)} %get-tuple-element.73), kind=kOutput, calls=%fused_computation.34 | convolution fusion | flops 2260992 | bytes 598016 | tf_op jit(solution)/shard_map/phtu,tphd->uphd/dot_general | solution.py:74
  61.2 1.8 copy.82
  63.3 1.8 copy.73
  65.1 1.0 reshape.205
  66.2 1.8 copy.75
  68.0 1.0 reshape.206
  69.2 2.1 convolution_multiply_fusion.4
  71.3 1.2 convolution_multiply_fusion.3
  72.5 2.6 %copy.77 = bf16[8,64,4,64]{1,0,3,2:T(8,128)(2,1)} copy(bf16[8,64,4,64]{3,0,2,1:T(8,128)(2,1)} %fusion.14) | data formatting | bytes 524288 | tf_op jit(solution)/shard_map/convert_element_type | solution.py:76
  75.0 2.1 reshape.207
  77.1 2.1 convolution_multiply_fusion.2
  79.2 3.0 %fusion.40 = (f32[512]{0:T(512)S(1)}, f32[512]{0:T(512)S(1)}, f32[512,512]{1,0:T(8,128)}) fusion(bf16[2,4,64,512]{3,2,0,1:T(8,128)(2,1)S(1)} %all-to-all-done, f32[512]{0:T(512)S(1)} %sqrt.9, f32[512]{0:T(512)S(1)} %copy-done.9, bf16[512,256]{1,0:T(8,128)(2,1)} %param.16, bf16[512,256]{1,0:T(8,128)(2,1)} %param.15, bf16[512,256]{1,0:T(8,128)(2,1)} %param.14, ...), kind=kOutput, calls=%fused_computation.80 | convolution fusion | flops 409205760 | bytes 3153920 | tf_op jit(solution)/shard_map/dot_general | solution.py:91
  82.5 1.1 copy-done.8
  83.6 1.1 multiply_convert_fusion
  84.7 3.5 %all-to-all-start.2 = ((bf16[8,1,64,512]{3,2,1,0:T(8,128)(2,1)}), bf16[8,1,64,512]{3,2,1,0:T(8,128)(2,1)S(1)}, u32[]{:S(2)}, u32[]{:S(2)}) async-start(bf16[8,1,64,512]{3,2,1,0:T(8,128)(2,1)} %multiply_convert_fusion), calls=%async_computation.2 | async-start | bytes 1048576 | tf_op jit(solution)/shard_map/all_to_all | solution.py:137
  88.2 1.1 fusion.16
  89.4 5.3 %all-to-all-done.2 = bf16[8,1,64,512]{3,2,1,0:T(8,128)(2,1)S(1)} async-done(((bf16[8,1,64,512]{3,2,1,0:T(8,128)(2,1)}), bf16[8,1,64,512]{3,2,1,0:T(8,128)(2,1)S(1)}, u32[]{:S(2)}, u32[]{:S(2)}) %all-to-all-start.2) | async-done | bytes 524320 | tf_op jit(solution)/shard_map/all_to_all | solution.py:137
  94.9 0.8 copy-done.4
  95.7 1.3 multiply_reduce_fusion
  97.2 3.5 %collective-permute-start.3 = (f32[2,8,1,512]{3,2,1,0:T(1,128)S(1)}, f32[2,8,1,512]{3,2,1,0:T(1,128)S(1)}, u32[]{:S(2)}, u32[]{:S(2)}) collective-permute-start(f32[2,8,1,512]{3,2,1,0:T(1,128)S(1)} %get-tuple-element.61), channel_id=1, source_target_pairs={{1,0},{2,1},{3,2},{4,3},{5,4},{6,5},{7,6},{0,7},{9,8},{10,9},{11,1... | collective-permute-start | bytes 98312 | tf_op jit(solution)/shard_map/ppermute | solution.py:22
  100.8 39.3 %all-reduce.2 = (f32[9,512]{1,0:T(8,128)}, f32[512]{0:T(512)}, f32[512]{0:T(512)}) all-reduce(f32[9,512]{1,0:T(8,128)S(1)} %broadcast_multiply_fusion, f32[512]{0:T(512)S(1)} %broadcast_multiply_fusion.2, f32[512]{0:T(512)S(1)} %broadcast_multiply_fusion.1), channel_id=1, replica_groups=mesh['sweep'=4,'azim'=8] {'sweep','azim'}, use_global_device_ids=true, to_apply=%region_14.15 | all-reduce | flops 5632 | bytes 45056 | tf_op jit(solution)/shard_map/psum | solution.py:181
  140.3 2.3 fusion.25
  142.6 88.1 %all-reduce.6.cloned.1.call-done = (f32[512,256]{1,0:T(8,128)}, f32[512,256]{1,0:T(8,128)}, f32[512,256]{1,0:T(8,128)}, f32[512,256]{0,1:T(8,128)}) async-done(((f32[512,256]{1,0:T(8,128)}, f32[512,256]{1,0:T(8,128)}, f32[512,256]{1,0:T(8,128)}, f32[512,256]{0,1:T(8,128)}), (f32[512,256]{1,0:T(8,128)}, f32[512,256]{1,0:T(8,128)}, f32[512,256]{1,0:T(8,128)}, ...) | async-done | bytes 2097168 | tf_op jit(solution)/shard_map/psum | solution.py:177
  230.7 1.0 constant_dynamic-slice_fusion
  231.7 0.7 copy.83
  232.4 1.5 constant_dynamic-slice_fusion.3
  233.9 1.5 constant_dynamic-slice_fusion.1
  (52 shorter events, 3.2 us)
Async XLA Ops:
  7.2 22.0 %copy-start = (bf16[512,256]{1,0:T(8,128)(2,1)S(1)}, bf16[512,256]{1,0:T(8,128)(2,1)}, u32[]{:S(2)}) copy-start(bf16[512,256]{1,0:T(8,128)(2,1)} %param.17) | copy-start | bytes 786436
  7.2 11.9 %copy-start.1 = (bf16[2,8,32,512]{3,2,1,0:T(8,128)(2,1)S(1)}, bf16[2,8,32,512]{3,2,1,0:T(8,128)(2,1)}, u32[]{:S(2)}) copy-start(bf16[2,8,32,512]{3,2,1,0:T(8,128)(2,1)} %param.9) | copy-start | bytes 1572868
  7.2 11.9 %copy-start.10 = (f32[9,512]{1,0:T(8,128)S(1)}, f32[9,512]{1,0:T(8,128)}, u32[]{:S(2)}) copy-start(f32[9,512]{1,0:T(8,128)} %param.11) | copy-start | bytes 55300
  8.3 10.8 %collective-permute-start = (bf16[2,8,1,512]{3,2,1,0:T(2,128)(2,1)S(1)}, bf16[2,8,1,512]{3,2,1,0:T(2,128)(2,1)S(1)}, u32[]{:S(2)}, u32[]{:S(2)}) collective-permute-start(bf16[2,8,1,512]{3,2,1,0:T(2,128)(2,1)S(1)} %get-tuple-element.62), channel_id=1, source_target_pairs={{0,1},{1,2},{2,3},{3,4},{4,5},{5,6},{6,7},{7,0},{8,9},{9,10},{10,1... | collective-permute-start | bytes 49160 | tf_op jit(solution)/shard_map/ppermute | solution.py:21
  8.8 10.3 %collective-permute-start.1 = (bf16[2,8,1,512]{3,2,1,0:T(2,128)(2,1)S(1)}, bf16[2,8,1,512]{3,2,1,0:T(2,128)(2,1)S(1)}, u32[]{:S(2)}, u32[]{:S(2)}) collective-permute-start(bf16[2,8,1,512]{3,2,1,0:T(2,128)(2,1)S(1)} %get-tuple-element.63), channel_id=1, source_target_pairs={{1,0},{2,1},{3,2},{4,3},{5,4},{6,5},{7,6},{0,7},{9,8},{10,9},{11,1... | collective-permute-start | bytes 49160 | tf_op jit(solution)/shard_map/ppermute | solution.py:22
  14.8 4.8 %copy-start.11 = (f32[512]{0:T(512)S(1)}, f32[512]{0:T(512)}, u32[]{:S(2)}) copy-start(f32[512]{0:T(512)} %param.12) | copy-start | bytes 6148
  14.8 10.9 %all-to-all-start.1 = ((bf16[2,4,64,512]{3,2,0,1:T(8,128)(2,1)}), bf16[2,4,64,512]{3,2,0,1:T(8,128)(2,1)S(1)}, u32[]{:S(2)}, u32[]{:S(2)}) async-start(bf16[2,4,64,512]{3,2,0,1:T(8,128)(2,1)} %copy.68), calls=%async_computation.1 | async-start | bytes 1048576 | tf_op jit(solution)/shard_map/all_to_all | solution.py:129
  21.3 14.6 %copy-start.9 = (f32[512]{0:T(512)S(1)}, f32[512]{0:T(512)}, u32[]{:S(2)}) copy-start(f32[512]{0:T(512)} %param.13) | copy-start | bytes 6148
  25.6 10.2 %copy-start.2 = (bf16[2,4,64,512]{3,2,0,1:T(8,128)(2,1)}, bf16[2,4,64,512]{3,2,0,1:T(8,128)(2,1)S(1)}, u32[]{:S(2)}) copy-start(bf16[2,4,64,512]{3,2,0,1:T(8,128)(2,1)S(1)} %all-to-all-done.1) | copy-start | bytes 1572868
  25.6 10.0 %all-to-all-start = ((bf16[2,4,64,512]{3,2,0,1:T(8,128)(2,1)}), bf16[2,4,64,512]{3,2,0,1:T(8,128)(2,1)S(1)}, u32[]{:S(2)}, u32[]{:S(2)}) async-start(bf16[2,4,64,512]{3,2,0,1:T(8,128)(2,1)} %copy.65), calls=%async_computation | async-start | bytes 1048576 | tf_op jit(solution)/shard_map/all_to_all | solution.py:128
  43.1 3.4 %copy-start.5 = (bf16[8,64,4,64]{3,2,1,0:T(4,128)(2,1)S(1)}, bf16[8,64,4,64]{3,2,1,0:T(4,128)(2,1)}, u32[]{:S(2)}) copy-start(bf16[8,64,4,64]{3,2,1,0:T(4,128)(2,1)} %reshape.203) | copy-start | bytes 786436
  46.4 2.9 %copy-start.6 = (bf16[8,64,4,64]{3,2,1,0:T(4,128)(2,1)S(1)}, bf16[8,64,4,64]{3,2,1,0:T(4,128)(2,1)}, u32[]{:S(2)}) copy-start(bf16[8,64,4,64]{3,2,1,0:T(4,128)(2,1)} %reshape.204) | copy-start | bytes 786436
  46.5 2.9 %copy-start.12 = (f32[64,4,8,8]{2,3,1,0:T(8,128)S(1)}, f32[64,4,8,8]{2,3,1,0:T(8,128)}, u32[]{:S(2)}) copy-start(f32[64,4,8,8]{2,3,1,0:T(8,128)} %get-tuple-element.74) | copy-start | bytes 196612
  69.0 2.3 copy-start.7
  82.3 1.2 copy-start.8
  83.6 4.6 %copy-start.3 = (bf16[2,4,64,512]{3,2,0,1:T(8,128)(2,1)S(1)}, bf16[2,4,64,512]{3,2,0,1:T(8,128)(2,1)}, u32[]{:S(2)}) copy-start(bf16[2,4,64,512]{3,2,0,1:T(8,128)(2,1)} %copy-done.2) | copy-start | bytes 1572868
  84.7 10.0 %all-to-all-start.2 = ((bf16[8,1,64,512]{3,2,1,0:T(8,128)(2,1)}), bf16[8,1,64,512]{3,2,1,0:T(8,128)(2,1)S(1)}, u32[]{:S(2)}, u32[]{:S(2)}) async-start(bf16[8,1,64,512]{3,2,1,0:T(8,128)(2,1)} %multiply_convert_fusion), calls=%async_computation.2 | async-start | bytes 1048576 | tf_op jit(solution)/shard_map/all_to_all | solution.py:137
  88.1 142.6 %all-reduce.6.cloned.1.call-start = ((), (), s32[]{:S(2)}) async-start(), calls=%async_computation.3 | async-start | bytes 4194304 | tf_op jit(solution)/shard_map/psum | solution.py:177
  94.7 1.0 copy-start.4
  97.1 43.0 %collective-permute-start.2 = (f32[2,8,1,512]{3,2,1,0:T(1,128)S(1)}, f32[2,8,1,512]{3,2,1,0:T(1,128)S(1)}, u32[]{:S(2)}, u32[]{:S(2)}) collective-permute-start(f32[2,8,1,512]{3,2,1,0:T(1,128)S(1)} %get-tuple-element.60), channel_id=1, source_target_pairs={{0,1},{1,2},{2,3},{3,4},{4,5},{5,6},{6,7},{7,0},{8,9},{9,10},{10,1... | collective-permute-start | bytes 98312 | tf_op jit(solution)/shard_map/ppermute | solution.py:21
  97.2 42.9 %collective-permute-start.3 = (f32[2,8,1,512]{3,2,1,0:T(1,128)S(1)}, f32[2,8,1,512]{3,2,1,0:T(1,128)S(1)}, u32[]{:S(2)}, u32[]{:S(2)}) collective-permute-start(f32[2,8,1,512]{3,2,1,0:T(1,128)S(1)} %get-tuple-element.61), channel_id=1, source_target_pairs={{1,0},{2,1},{3,2},{4,3},{5,4},{6,5},{7,6},{0,7},{9,8},{10,9},{11,1... | collective-permute-start | bytes 98312 | tf_op jit(solution)/shard_map/ppermute | solution.py:22
Sparse Core Ops, SparseCore 0:
  94.6 136.0 all-reduce.5
where the time goes:
time: 243 us; the launch traced here: 242 us
  waiting for transfers between devices  103 us (42%)
  blocking collectives  39.3 us (16%)
  matrix products  31.6 us (13%)
  local copies, waits for them, and re-layouts  27.5 us (11%)
  starting transfers between devices  19.5 us (8%)
  between operations  14.3 us (6%)
  other arithmetic  7.1 us (3%)
    psum x1, waiting for transfers between devices, on_device(): lax.psum((query_terms, key_terms, value_terms, output_terms), ('sweep', '...  88.1 us
    psum x1, blocking collectives, on_device(): lax.psum((tap_terms, bias_terms, gain_terms), ('sweep', 'azim'))  39.3 us
    ppermute x2, starting transfers between devices, extended(): after = lax.ppermute(leading, axis, down)  7.63 us
    dot_general x4, matrix products, outer_sum(): lax.dot_general(left, right, (((0,), (0,)), ((), ())), preferred_element_...  6.46 us
    all_to_all x1, waiting for transfers between devices, on_device(): lax.all_to_all(grad_attn.reshape(total_sweeps, 1, pixels_each, channels),...  5.34 us
    all_to_all x1, waiting for transfers between devices, on_device(): lax.all_to_all(y_split, 'sweep', split_axis=1, concat_axis=0, tiled=True)  5.19 us
  transfers between devices with their start and end apart: 8, of which 4 were waited for; matrix products, arithmetic and copies ran while one was open for 4% of the time, Pallas kernels for 0%

commit v1 on v0

v1 whole, which is shorter than its diff:
```python
import functools
import math

import jax
import jax.numpy as jnp
from jax import lax
from jax.experimental import pallas as pl
from jax.experimental.pallas import tpu as pltpu
from jax.sharding import PartitionSpec as P

DH = 64
EPS = 1e-06
LANES = 128
PIX = 16
MESH = pl.DeviceIdType.MESH
VMEM = pl.BlockSpec(memory_space=pltpu.VMEM)
BIG = 56 * 1024 * 1024


def remote(src, dst, send, recv, where):
    return pltpu.make_async_remote_copy(
        src_ref=src, dst_ref=dst, send_sem=send, recv_sem=recv, device_id=where, device_id_type=MESH
    )


def greet(partners):
    barrier = pltpu.get_barrier_semaphore()
    for where in partners:
        pl.semaphore_signal(barrier, inc=1, device_id=where, device_id_type=MESH)
    pl.semaphore_wait(barrier, len(partners))


def store_shifted(dst, s, h, val):
    width = val.shape[0]
    dst[1, s, h + 1] = val
    dst[0, s, h + 1] = pltpu.roll(val, 1, 0)
    dst[2, s, h + 1] = pltpu.roll(val, width - 1, 0)


def patch_edges(dst, left, right, sweeps, height, width):
    for s in range(sweeps):
        for h in range(height):
            i = s * height + h
            dst[0, s, h + 1, 0:1, :] = left[i : i + 1, :]
            dst[2, s, h + 1, width - 1 : width, :] = right[i : i + 1, :]


def zero_frame(dst, sweeps, height):
    for b in range(3):
        for s in range(sweeps):
            dst[b, s, 0] = jnp.zeros(dst.shape[3:], jnp.float32)
            dst[b, s, height + 1] = jnp.zeros(dst.shape[3:], jnp.float32)


def forward_kernel(
    groups, strips, lat, cot, kern, bias, y_pix, cot_pix, halo_left, halo_right,
    act, y_src, edge_left, edge_right, a2a_send, a2a_recv, own_sem, halo_send, halo_recv,
):
    sweeps, height, width, channels = lat.shape
    each = height * width // groups
    me = lax.axis_index("sweep")
    az = lax.axis_index("azim")
    right, left = lax.rem(az + 1, strips), lax.rem(az + strips - 1, strips)
    partners = [lax.rem(me + k, groups) for k in range(1, groups)]
    greet([{"sweep": g} for g in partners] + [{"azim": left}, {"azim": right}])
    mine = pl.ds(pl.multiple_of(me * each, PIX), each)
    slots = pl.ds(me * sweeps, sweeps)

    def sends(src, out, at):
        copies = []
        for k, g in enumerate(partners):
            there = pl.ds(pl.multiple_of(g * each, PIX), each)
            copies.append(
                remote(src.at[:, there, :], out.at[slots], a2a_send.at[at, k], a2a_recv.at[at, k], {"sweep": g})
            )
        for copy in copies:
            copy.start()
        own = pltpu.make_async_copy(src.at[:, mine, :], out.at[slots], own_sem.at[at])
        own.start()
        return copies, own

    cot_copies, cot_own = sends(cot, cot_pix, 0)

    for s in range(sweeps):
        def activate(h, carry, s=s):
            x = lat[s, h].astype(jnp.float32)
            val = x / (1.0 + jnp.exp(-x))
            store_shifted(act, s, h, val)
            edge_left[pl.ds(s * height + h, 1), :] = val[0:1]
            edge_right[pl.ds(s * height + h, 1), :] = val[width - 1 : width]
            return carry
        lax.fori_loop(0, height, activate, 0)
    to_right = remote(edge_right, halo_left, halo_send.at[0], halo_recv.at[0], {"azim": right})
    to_left = remote(edge_left, halo_right, halo_send.at[1], halo_recv.at[1], {"azim": left})
    to_right.start()
    to_left.start()
    zero_frame(act, sweeps, height)
    to_right.wait()
    to_left.wait()
    patch_edges(act, halo_left, halo_right, sweeps, height, width)
    for s in range(sweeps):
        def convolve(h, carry, s=s):
            total = lat[s, h].astype(jnp.float32) + bias[...]
            for a in range(3):
                for b in range(3):
                    total = total + kern[3 * a + b : 3 * a + b + 1, :] * act[b, s, h + a]
            y_src[s, pl.ds(pl.multiple_of(h * width, PIX), width), :] = total.astype(jnp.bfloat16)
            return carry
        lax.fori_loop(0, height, convolve, 0)
    y_copies, y_own = sends(y_src, y_pix, 1)
    for copy in cot_copies + y_copies:
        copy.wait()
    cot_own.wait()
    y_own.wait()


def dot(a, b, dims):
    return lax.dot_general(a, b, (dims, ((), ())), preferred_element_type=jnp.float32)


NN = ((1,), (0,))
NT = ((1,), (1,))
TN = ((0,), (0,))


def attend_kernel(
    heads, y_ref, cot_ref, gain_ref, wq_ref, wk_ref, wv_ref, wo_ref, grad_ref, mats_ref, gain_out,
    rows_s, cot_s, att_s, gq_s, gk_s, gv_s,
):
    sweeps, pixels, channels = y_ref.shape
    inner = wq_ref.shape[1]
    m = sweeps * PIX
    scale = 1.0 / math.sqrt(DH)
    gain = gain_ref[...]
    wq, wk, wv, wo = wq_ref[...], wk_ref[...], wv_ref[...], wo_ref[...]
    row_pix = lax.broadcasted_iota(jnp.int32, (m, m), 0) % PIX
    col_pix = lax.broadcasted_iota(jnp.int32, (m, m), 1) % PIX
    same = row_pix == col_pix
    same = jnp.concatenate([same] * heads, axis=0)
    lane_head = lax.broadcasted_iota(jnp.int32, (1, inner), 1) // DH

    def spread(value):
        return jnp.concatenate(
            [jnp.where(lane_head == h, value, jnp.zeros_like(value)) for h in range(heads)], axis=0
        )

    def collect(value):
        total = jnp.where(lane_head == 0, value[0:m], 0.0)
        for h in range(1, heads):
            total = jnp.where(lane_head == h, value[h * m : (h + 1) * m], total)
        return total

    gain_total = jnp.zeros((1, channels), jnp.float32)
    for block in range(pixels // PIX):
        at = slice(block * PIX, (block + 1) * PIX)
        own = slice(block * m, (block + 1) * m)
        y = y_ref[:, at, :].reshape(m, channels).astype(jnp.float32)
        cot = cot_ref[:, at, :].reshape(m, channels)
        root = jnp.sqrt(jnp.mean(y * y, axis=-1, keepdims=True) + EPS)
        inverse = 1.0 / root
        normed = (y * inverse * gain).astype(jnp.bfloat16)
        rows_s[own, :] = normed
        cot_s[own, :] = cot
        query = dot(normed, wq, NN).astype(jnp.bfloat16)
        key = dot(normed, wk, NN).astype(jnp.bfloat16)
        value = dot(normed, wv, NN).astype(jnp.bfloat16)
        grad_att = dot(cot, wo, NN).astype(jnp.bfloat16)
        query_x = spread(query)
        grad_att_x = spread(grad_att)
        scores = jnp.where(same, dot(query_x, key, NT) * scale, -1e30)
        top = jnp.max(scores, axis=-1, keepdims=True)
        expon = jnp.exp(scores - top)
        probs = expon / jnp.sum(expon, axis=-1, keepdims=True)
        probs_low = probs.astype(jnp.bfloat16)
        att_s[own, :] = collect(dot(probs_low, value, NN)).astype(jnp.bfloat16)
        grad_probs = dot(grad_att_x, value, NT)
        inner_sum = jnp.sum(probs * grad_probs, axis=-1, keepdims=True)
        grad_scores = (probs * (grad_probs - inner_sum) * scale).astype(jnp.bfloat16)
        grad_v = dot(probs_low, grad_att_x, TN).astype(jnp.bfloat16)
        grad_q = collect(dot(grad_scores, key, NN)).astype(jnp.bfloat16)
        grad_k = dot(grad_scores, query_x, TN).astype(jnp.bfloat16)
        gq_s[own, :] = grad_q
        gk_s[own, :] = grad_k
        gv_s[own, :] = grad_v
        grad_normed = dot(grad_q, wq, NT) + dot(grad_k, wk, NT) + dot(grad_v, wv, NT)
        gain_total = gain_total + jnp.sum(grad_normed * y * inverse, axis=0, keepdims=True)
        gained = grad_normed * gain
        mean = jnp.mean(gained * y, axis=-1, keepdims=True)
        grad = inverse * (gained - y * mean * inverse * inverse)
        grad_ref[:, at, :] = grad.astype(jnp.bfloat16).reshape(sweeps, PIX, channels)
    gain_out[...] = gain_total
    per = inner // LANES
    for i, (left, right) in enumerate(
        ((rows_s, gq_s), (rows_s, gk_s), (rows_s, gv_s), (cot_s, att_s))
    ):
        full = dot(left[...], right[...], TN)
        for j in range(per):
            mats_ref[i * per + j] = full[:, j * LANES : (j + 1) * LANES]


def backward_kernel(
    groups, strips, predivide, grad, mats, cot, lat, kern, halo_left, halo_right, gain,
    out_lat, out_small, out_q, out_k, out_v, out_o,
    act, gy, ret, edge_left, edge_right, in_left, in_right, taps,
    pair_buf, acc, sweep_buf, acc2, z_buf, fin,
    small, small_pair, small_sweep, small_z,
    a2a_send, a2a_recv, own_sem, halo_send, halo_recv, pair_send, pair_recv,
    sweep_send, sweep_recv, z_send, z_recv, fin_send, fin_recv,
    sp_send, sp_recv, ss_send, ss_recv, sz_send, sz_recv,
):
    sweeps, height, width, channels = lat.shape
    each = height * width // groups
    planes = strips // 2
    me = lax.axis_index("sweep")
    az = lax.axis_index("azim")
    core = lax.rem(az, 2)
    z = az // 2
    other = az + 1 - 2 * core
    right, left = lax.rem(az + 1, strips), lax.rem(az + strips - 1, strips)
    partners = [lax.rem(me + k, groups) for k in range(1, groups)]
    z_partners = [lax.rem(z + k, planes) for k in range(1, planes)]
    greet(
        [{"sweep": g} for g in partners]
        + [{"azim": left}, {"azim": right}, {"azim": other}]
        + [{"azim": p * 2 + core} for p in z_partners]
    )
    mine = pl.ds(pl.multiple_of(me * each, PIX), each)
    slots = pl.ds(me * sweeps, sweeps)
    back = []
    for k, g in enumerate(partners):
        back.append(
            remote(grad.at[pl.ds(g * sweeps, sweeps)], ret.at[:, mine, :], a2a_send.at[k], a2a_recv.at[k], {"sweep": g})
        )
    for copy in back:
        copy.start()
    pair = remote(mats.at[:, :, 1 - core], pair_buf, pair_send, pair_recv, {"azim": other})
    pair.start()
    own = pltpu.make_async_copy(grad.at[slots], ret.at[:, mine, :], own_sem)
    own.start()

    for s in range(sweeps):
        def activate(h, carry, s=s):
            x = lat[s, h].astype(jnp.float32)
            store_shifted(act, s, h, x / (1.0 + jnp.exp(-x)))
            return carry
        lax.fori_loop(0, height, activate, 0)
    zero_frame(act, sweeps, height)
    zero_frame(gy, sweeps, height)
    patch_edges(act, halo_left, halo_right, sweeps, height, width)
    taps[...] = jnp.zeros(taps.shape, jnp.float32)

    for copy in back:
        copy.wait()
    own.wait()
    for s in range(sweeps):
        def combine(h, carry, s=s):
            got = ret[s, pl.ds(pl.multiple_of(h * width, PIX), width), :]
            val = cot[s, h].astype(jnp.float32) + got.astype(jnp.float32)
            store_shifted(gy, s, h, val)
            edge_left[pl.ds(s * height + h, 1), :] = val[0:1]
            edge_right[pl.ds(s * height + h, 1), :] = val[width - 1 : width]
            return carry
        lax.fori_loop(0, height, combine, 0)
    to_right = remote(edge_right, in_left, halo_send.at[0], halo_recv.at[0], {"azim": right})
    to_left = remote(edge_left, in_right, halo_send.at[1], halo_recv.at[1], {"azim": left})
    to_right.start()
    to_left.start()

    pair.wait()
    chunks, _, _, parts, rows, _ = mats.shape
    def add_pair(c, carry):
        for p in range(parts):
            for q in range(planes):
                acc[c * parts + p, q] = mats[c, q, core, p] + pair_buf[c, q, p]
        return carry
    lax.fori_loop(0, chunks, add_pair, 0)
    per = chunks * parts // groups
    scatter = []
    for k, g in enumerate(partners):
        scatter.append(
            remote(acc.at[pl.ds(g * per, per)], sweep_buf.at[k], sweep_send.at[k], sweep_recv.at[k], {"sweep": g})
        )
    for copy in scatter:
        copy.start()

    to_right.wait()
    to_left.wait()
    patch_edges(gy, in_left, in_right, sweeps, height, width)
    for s in range(sweeps):
        def convolve(h, carry, s=s):
            mid = gy[1, s, h + 1]
            total = jnp.zeros(mid.shape, jnp.float32)
            def fold(v):
                return sum(v[8 * i : 8 * i + 8] for i in range(1, width // 8)) + v[0:8]
            for a in range(3):
                for b in range(3):
                    t = 3 * a + b
                    total = total + kern[t : t + 1, :] * gy[2 - b, s, h + 2 - a]
                    taps[t] = taps[t] + fold(mid * act[b, s, h + a])
            taps[9] = taps[9] + fold(mid)
            x = lat[s, h].astype(jnp.float32)
            sig = 1.0 / (1.0 + jnp.exp(-x))
            out_lat[s, h] = mid + total * (sig * (1.0 + x * (1.0 - sig)))
            return carry
        lax.fori_loop(0, height, convolve, 0)
    small[...] = jnp.zeros(small.shape, jnp.float32)
    for t in range(10):
        small[t : t + 1, :] = jnp.sum(taps[t], axis=0, keepdims=True) * predivide
    small[10:11, :] = gain[...] * predivide
    sp = remote(small, small_pair, sp_send, sp_recv, {"azim": other})
    sp.start()

    for copy in scatter:
        copy.wait()
    for i in range(per):
        def add_sweep(q, carry, i=i):
            total = acc[me * per + i, q]
            for k in range(groups - 1):
                total = total + sweep_buf[k, i, q]
            acc2[q, i] = total
            return carry
        lax.fori_loop(0, planes, add_sweep, 0)
    along = []
    for k, p in enumerate(z_partners):
        along.append(
            remote(acc2.at[p], z_buf.at[k], z_send.at[k], z_recv.at[k], {"azim": p * 2 + core})
        )
    for copy in along:
        copy.start()

    sp.wait()
    small_sweep[me] = small[...] + small_pair[...]
    ss = []
    for k, g in enumerate(partners):
        ss.append(
            remote(small_sweep.at[me], small_sweep.at[me], ss_send.at[k], ss_recv.at[k], {"sweep": g})
        )
    for copy in ss:
        copy.start()

    for copy in along:
        copy.wait()
    for i in range(per):
        total = acc2[z, i]
        for k in range(planes - 1):
            total = total + z_buf[k, i]
        fin[me, i] = total * predivide
    gather = []
    for k, g in enumerate(partners):
        gather.append(
            remote(fin.at[me], fin.at[me], fin_send.at[k], fin_recv.at[k], {"sweep": g})
        )
    for copy in gather:
        copy.start()
    for copy in ss:
        copy.wait()
    total = small_sweep[0]
    for g in range(1, groups):
        total = total + small_sweep[g]
    small_z[z] = total
    sz = []
    for k, p in enumerate(z_partners):
        sz.append(
            remote(small_z.at[z], small_z.at[z], sz_send.at[k], sz_recv.at[k], {"azim": p * 2 + core})
        )
    for copy in sz:
        copy.start()
    for copy in gather:
        copy.wait()
    lanes = chunks // 4
    for g in range(groups):
        for i in range(per):
            c, p = divmod(g * per + i, parts)
            out = (out_q, out_k, out_v, out_o)[c // lanes]
            j = c % lanes
            out[p * rows : (p + 1) * rows, j * LANES : (j + 1) * LANES] = fin[g, i]
    for copy in sz:
        copy.wait()
    total = small_z[0]
    for p in range(1, planes):
        total = total + small_z[p]
    out_small[...] = total


def on_device(
    latents, cotangent, conv_kernel, conv_bias, norm_gain, w_query, w_key, w_value, w_output
):
    f32, bf16 = jnp.float32, jnp.bfloat16
    dma = pltpu.SemaphoreType.DMA
    sds = jax.ShapeDtypeStruct
    sweeps, height, width, channels = latents.shape
    inner = w_query.shape[1]
    groups = lax.axis_size("sweep")
    strips = lax.axis_size("azim")
    planes = strips // 2
    each = height * width // groups
    total = sweeps * groups
    tokens = total * each
    lines = sweeps * height
    edge = pltpu.VMEM((lines, channels), f32)
    framed = pltpu.VMEM((3, sweeps, height + 2, width, channels), f32)
    flat = (sweeps, height * width, channels)

    y_pix, cot_pix, halo_left, halo_right = pl.pallas_call(
        functools.partial(forward_kernel, groups, strips),
        out_shape=[
            sds((total, each, channels), bf16),
            sds((total, each, channels), bf16),
            sds((lines, channels), f32),
            sds((lines, channels), f32),
        ],
        in_specs=[VMEM] * 4,
        out_specs=[VMEM] * 4,
        scratch_shapes=[
            framed, pltpu.VMEM(flat, bf16), edge, edge,
            dma((2, groups - 1)), dma((2, groups - 1)), dma((2,)), dma((2,)), dma((2,)),
        ],
        compiler_params=pltpu.CompilerParams(
            collective_id=0, has_side_effects=True, vmem_limit_bytes=BIG
        ),
        name="conv_forward",
    )(latents, cotangent.reshape(flat), conv_kernel, conv_bias.reshape(1, channels))

    chunks = 4 * inner // LANES
    grad_attn, mats, gain = pl.pallas_call(
        functools.partial(attend_kernel, inner // DH),
        out_shape=[
            sds((total, each, channels), bf16),
            sds((chunks, channels, LANES), f32),
            sds((1, channels), f32),
        ],
        in_specs=[VMEM] * 7,
        out_specs=[VMEM] * 3,
        scratch_shapes=[
            pltpu.VMEM((tokens, channels), bf16),
            pltpu.VMEM((tokens, channels), bf16),
            pltpu.VMEM((tokens, inner), bf16),
            pltpu.VMEM((tokens, inner), bf16),
            pltpu.VMEM((tokens, inner), bf16),
            pltpu.VMEM((tokens, inner), bf16),
        ],
        compiler_params=pltpu.CompilerParams(vmem_limit_bytes=BIG),
        name="attend",
    )(y_pix, cot_pix, norm_gain.reshape(1, channels), w_query, w_key, w_value, w_output)

    rows_each = channels // strips
    parts = max(1, groups // chunks)
    rows = rows_each // parts
    per = chunks * parts // groups
    predivide = 1.0 / math.sqrt(total * height * width * strips)
    small_shape = (16, channels)
    out_mat = sds((rows_each, inner), f32)
    grad_latents, small, gq, gk, gv, go = pl.pallas_call(
        functools.partial(backward_kernel, groups, strips, predivide),
        out_shape=[
            sds(latents.shape, f32), sds(small_shape, f32), out_mat, out_mat, out_mat, out_mat,
        ],
        in_specs=[VMEM] * 8,
        out_specs=[VMEM] * 6,
        scratch_shapes=[
            framed, framed, pltpu.VMEM(flat, bf16), edge, edge, edge, edge,
            pltpu.VMEM((10, 8, channels), f32),
            pltpu.VMEM((chunks, planes, parts, rows, LANES), f32),
            pltpu.VMEM((chunks * parts, planes, rows, LANES), f32),
            pltpu.VMEM((groups - 1, per, planes, rows, LANES), f32),
            pltpu.VMEM((planes, per, rows, LANES), f32),
            pltpu.VMEM((planes - 1, per, rows, LANES), f32),
            pltpu.VMEM((groups, per, rows, LANES), f32),
            pltpu.VMEM(small_shape, f32),
            pltpu.VMEM(small_shape, f32),
            pltpu.VMEM((groups,) + small_shape, f32),
            pltpu.VMEM((planes,) + small_shape, f32),
            dma((groups - 1,)), dma((groups - 1,)), dma(()), dma((2,)), dma((2,)), dma(()), dma(()),
            dma((groups - 1,)), dma((groups - 1,)), dma((planes - 1,)), dma((planes - 1,)),
            dma((groups - 1,)), dma((groups - 1,)),
            dma(()), dma(()), dma((groups - 1,)), dma((groups - 1,)),
            dma((planes - 1,)), dma((planes - 1,)),
        ],
        compiler_params=pltpu.CompilerParams(
            collective_id=1, has_side_effects=True, vmem_limit_bytes=BIG
        ),
        name="conv_backward",
    )(
        grad_attn, mats.reshape(chunks, planes, 2, parts, rows, LANES), cotangent, latents,
        conv_kernel, halo_left, halo_right, gain,
    )
    return (grad_latents, small[:9], small[9], small[10], gq, gk, gv, go)


def solution(mesh):
    image = P("sweep", None, "azim", None)
    share = P("azim", None)
    return jax.shard_map(
        on_device,
        mesh=mesh,
        in_specs=(image, image) + (P(),) * 7,
        out_specs=(image, P(), P(), P(), share, share, share, share),
        check_vma=False,
    )
```

time: 243 us -> 73.4 us (0.30)
  waiting for transfers between devices: 103 us -> 0 us
  Pallas kernels: 0 us -> 65.6 us
  blocking collectives: 39.3 us -> 0 us
  matrix products: 31.6 us -> 0 us
  local copies, waits for them, and re-layouts: 27.5 us -> 6.84 us
  starting transfers between devices: 19.5 us -> 0 us
  between operations: 14.3 us -> 0.69 us
  other arithmetic: 7.1 us -> 0 us
    psum x1 -> x0, waiting for transfers between devices: 88.1 us -> none  [on_device(): lax.psum((query_terms, key_terms, value_terms, output_terms), ('sweep', '...]
    pallas_call x0 -> x3, Pallas kernels: none -> 65.6 us  [the longest x1 38.1 us: on_device(): pl.pallas_call(functools.partial(backward_kernel, groups, strips, predivi...]
    psum x1 -> x0, blocking collectives: 39.3 us -> none  [on_device(): lax.psum((tap_terms, bias_terms, gain_terms), ('sweep', 'azim'))]
    dot_general x14 -> x0, matrix products: 28.3 us -> none  [the longest x4 6.46 us: outer_sum(): lax.dot_general(left, right, (((0,), (0,)), ((), ())), preferred_element_...]
    all_to_all x3 -> x0, waiting for transfers between devices: 14.8 us -> none  [the longest x1 5.34 us: on_device(): lax.all_to_all(grad_attn.reshape(total_sweeps, 1, pixels_each, channels),...]
    reshape x10 -> x0, local copies, waits for them, and re-layouts: 11.4 us -> none  [the longest x1 2.08 us: attend(): grad_v = grad_v.reshape(sweeps * pixels, heads * DH)]
    all_to_all x3 -> x0, starting transfers between devices: 11.2 us -> none  [the longest x1 4.28 us: on_device(): lax.all_to_all(cot_split, 'sweep', split_axis=1, concat_axis=0, tiled=True)]
    ppermute x4 -> x0, starting transfers between devices: 8.2 us -> none  [the longest x2 7.63 us: extended(): after = lax.ppermute(leading, axis, down)]
  transfers between devices with their start and end apart: 8 -> 0, of which waited for: 4 -> 0; matrix products, arithmetic and copies ran while one was open for 4% -> 0% of each run, Pallas kernels for 0% -> 0%
where the time goes in v1:
time: 73.4 us; the launch traced here: 73.2 us
  Pallas kernels  65.6 us (89%)
  local copies, waits for them, and re-layouts  6.84 us (9%)
    pallas_call x1, Pallas kernels, on_device(): pl.pallas_call(functools.partial(backward_kernel, groups, strips, predivi...  38.1 us
    pallas_call x1, Pallas kernels, on_device(): pl.pallas_call(functools.partial(forward_kernel, groups, strips), out_sha...  19.3 us
    pallas_call x1, Pallas kernels, on_device(): pl.pallas_call(functools.partial(attend_kernel, inner // DH), out_shape=[...  8.3 us
    unnamed x16, local copies, waits for them, and re-layouts  5.44 us

profile of v1, /device:TPU:0, one launch (start us, length us, event | category | flops | bytes accessed | tf_op | source)
XLA Modules:
  0.0 73.2 jit_solution(4511426418145692701)
XLA Ops:
  0.6 19.3 %conv_forward.1 = (bf16[8,64,512]{2,1,0:T(8,128)(2,1)}, bf16[8,64,512]{2,1,0:T(8,128)(2,1)}, f32[16,512]{1,0:T(8,128)}, f32[16,512]{1,0:T(8,128)}) custom-call(bf16[2,8,32,512]{3,2,1,0:T(8,128)(2,1)} %lat.3, bf16[2,256,512]{2,1,0:T(8,128)(2,1)} %bitcast.7, f32[9,512]{1,0:T(8,128)} %kern.3, f32[1,512]{1,0:T(1,128)} %bitcast.10), custom_call_target="tpu_custom_call" | custom-call | tf_op jit(solution)/shard_map/conv_forward/pallas_call | solution.py:404
  19.9 8.3 %attend.1 = (bf16[8,64,512]{2,1,0:T(8,128)(2,1)}, f32[8,512,128]{2,1,0:T(8,128)}, f32[1,512]{1,0:T(1,128)}) custom-call(bf16[8,64,512]{2,1,0:T(8,128)(2,1)} %get-tuple-element.21.y_ref, bf16[8,64,512]{2,1,0:T(8,128)(2,1)} %get-tuple-element.22.cot_ref, f32[1,512]{1,0:T(1,128)} %bitcast.11, bf16[512,256]{1,0:T(8,128)(2,1)} %wq_ref.1, ...), custom_call_target="tpu_custom_call" | custom-call | tf_op jit(solution)/shard_map/attend/pallas_call | solution.py:425
  28.2 38.1 %conv_backward.1 = (f32[2,8,32,512]{3,2,1,0:T(8,128)}, f32[16,512]{1,0:T(8,128)}, f32[64,256]{1,0:T(8,128)}, f32[64,256]{1,0:T(8,128)}, f32[64,256]{1,0:T(8,128)}, /*index=5*/f32[64,256]{1,0:T(8,128)}) custom-call(bf16[8,64,512]{2,1,0:T(8,128)(2,1)} %get-tuple-element.23.grad, f32[8,4,2,1,64,128]{5,4,3,2,1,0:T(8,128)} %bitcast.8, ...), custom_call_target="tpu_custom_call" | custom-call | tf_op jit(solution)/shard_map/conv_backward/pallas_call | solution.py:453
  66.3 0.0 copy-start.4
  66.3 0.0 copy-start.3
  66.3 0.0 copy-start.2
  66.3 0.0 copy-start.1
  66.3 0.0 copy-start
  66.3 1.4 %fusion = (f32[1,512]{1,0:T(1,128)}, f32[1,512]{1,0:T(1,128)}) fusion(f32[16,512]{1,0:T(8,128)} %get-tuple-element.29), kind=kLoop, calls=%fused_computation | loop fusion | bytes 8192 | tf_op jit(solution)/shard_map/slice | solution.py:487
  67.7 2.3 %copy.23 = f32[2,8,32,512]{3,2,1,0:T(8,128)} copy(f32[2,8,32,512]{3,2,1,0:T(8,128)} %get-tuple-element.44) | data formatting | bytes 2097152
  70.0 0.0 copy-done.4
  70.0 0.6 copy.24
  70.6 0.0 copy-done.3
  70.6 0.6 copy.25
  71.3 0.0 copy-done.2
  71.3 0.6 copy.26
  71.9 0.0 copy-done.1
  71.9 0.6 copy.27
  72.5 0.0 copy-done
  72.5 0.6 copy.28
Async XLA Ops:
  66.3 3.7 %copy-start.4 = (f32[16,512]{1,0:T(8,128)S(1)}, f32[16,512]{1,0:T(8,128)}, u32[]{:S(2)}) copy-start(f32[16,512]{1,0:T(8,128)} %get-tuple-element.29) | copy-start | bytes 98308
  66.3 4.3 %copy-start.3 = (f32[64,256]{1,0:T(8,128)S(1)}, f32[64,256]{1,0:T(8,128)}, u32[]{:S(2)}) copy-start(f32[64,256]{1,0:T(8,128)} %get-tuple-element.48) | copy-start | bytes 196612
  66.3 5.0 %copy-start.2 = (f32[64,256]{1,0:T(8,128)S(1)}, f32[64,256]{1,0:T(8,128)}, u32[]{:S(2)}) copy-start(f32[64,256]{1,0:T(8,128)} %get-tuple-element.49) | copy-start | bytes 196612
  66.3 5.6 %copy-start.1 = (f32[64,256]{1,0:T(8,128)S(1)}, f32[64,256]{1,0:T(8,128)}, u32[]{:S(2)}) copy-start(f32[64,256]{1,0:T(8,128)} %get-tuple-element.50) | copy-start | bytes 196612
  66.3 6.2 %copy-start = (f32[64,256]{1,0:T(8,128)S(1)}, f32[64,256]{1,0:T(8,128)}, u32[]{:S(2)}) copy-start(f32[64,256]{1,0:T(8,128)} %get-tuple-element.51) | copy-start | bytes 196612
